TPU v7x, 32 devices: a whole 2x2x4 slice. The times are simulated.
32 devices in a mesh: dp: 8 (over y, x, core), mp: 4 (over z).
Axes of the slice: x: 2, y: 2, z: 4, core: 2. Of those that a mesh axis runs over, the one named last changes fastest.
Arguments:
- tokens: bfloat16 [4096, 4096], P('dp'), may hold values from -6 to 6
- cache: bfloat16 [192, 128, 896], P('dp'), may hold values from -220 to 220
- nb_row: int32 [64, 2], P('dp'), may hold values from 0 to 23
- nb_owner: int32 [64, 2], P('dp'), may hold values from 0 to 7, all different within a row; in each aligned block of 8 rows (0 to 7, 8 to 15, ...) at most 3 rows name the same one
- nb_len: int32 [64, 2], P('dp'), may hold values from 32 to 128, as said below
- w_query: bfloat16 [4096, 4096], P('dp', 'mp'), may hold values from -0.09375 to 0.09375
- w_key: bfloat16 [896, 4096], P('dp', 'mp'), may hold values from -0.1875 to 0.1875
- w_value: bfloat16 [896, 4096], P('dp', 'mp'), may hold values from -0.1875 to 0.1875
- w_out: bfloat16 [4096, 4096], P('mp', 'dp'), may hold values from -0.09375 to 0.09375
- grad_out: bfloat16 [4096, 4096], P('dp'), may hold values from -6 to 6
Outputs:
- mixed: bfloat16 [4096, 4096], P('dp', 'mp')
- grad_tokens: bfloat16 [4096, 4096], P('dp', 'mp')
- grad_query: float32 [4096, 4096], P('dp', 'mp')
- grad_key: float32 [896, 4096], P('dp', 'mp')
- grad_value: float32 [896, 4096], P('dp', 'mp')
- grad_wout: float32 [4096, 4096], P('mp', 'dp')
Inputs may be any that keep to these rules, and one draw needn't show every extreme that they name: `nb_owner`: among the 8 stretches of one index of dp no shard is named more than 3 times, a bound that some block reaches; the 2 neighbours of a stretch lie on different shards. `nb_len`: the first neighbour of every stretch has all 128 tokens.
All inputs are finite; a program needn't handle non-finite values.
Results may differ from a plain program's by a relative error of at most 0.014.
The roundings to bfloat16 on the way count: a program that leaves them out, or rounds other values in their place, can miss the bound.
Values may be sent and summed in bfloat16 or wider, within the bound.
A program may use at most 128 MiB of HBM per device.

v0:
```python
import jax
import jax.numpy as jnp
from jax import lax
from jax.sharding import PartitionSpec as P

HD = 128
CL = 64
KN = 2
CAP = 3


def on_device(tokens, cache, nb_row, nb_owner, nb_len, w_query, w_key, w_value, w_out, grad_out):
    dp_count = lax.axis_size("dp")
    mp_count = lax.axis_size("mp")
    mp_place = lax.axis_index("mp")
    tok_rows, width = tokens.shape
    head_span = w_query.shape[1]
    heads_here = head_span // HD
    stretch_count = nb_row.shape[0]
    request_count = stretch_count * KN
    cache_rows, block_len, enc_width = cache.shape
    width_share = width // mp_count
    score_scale = HD ** (-0.5)
    wide_tokens = tokens.astype(jnp.float32)
    inv_rms = lax.rsqrt(jnp.mean(wide_tokens * wide_tokens, axis=1, keepdims=True) + 1e-06)
    normed_wide = wide_tokens * inv_rms
    normed = normed_wide.astype(jnp.bfloat16)
    query_full = lax.all_gather(w_query, "dp", axis=0, tiled=True)
    output_full = lax.all_gather(w_out, "dp", axis=1, tiled=True)
    queries = jnp.dot(normed, query_full, preferred_element_type=jnp.float32).astype(jnp.bfloat16)
    owners = nb_owner.reshape(-1)
    wanted = nb_row.reshape(-1)
    req_order = jnp.arange(request_count)
    earlier = (owners[:, None] == owners[None, :]) & (req_order[None, :] < req_order[:, None])
    rank_seen = jnp.sum(earlier.astype(jnp.int32), axis=1)
    slot_of = owners * CAP + rank_seen
    slot_hits = (slot_of[:, None] == jnp.arange(dp_count * CAP)[None, :]).astype(jnp.int32)
    asked_ids = (jnp.sum(slot_hits * (wanted[:, None] + 1), axis=0) - 1).reshape(dp_count, CAP)
    picked_rows = jnp.clip(
        lax.all_to_all(asked_ids, "dp", split_axis=0, concat_axis=0, tiled=True), 0, cache_rows - 1
    )
    picked = jnp.take(cache, picked_rows, axis=0)
    arrived = lax.all_to_all(picked, "dp", split_axis=0, concat_axis=0, tiled=True)
    arrived = arrived.reshape(dp_count * CAP, arrived.shape[2], enc_width)
    blocks = jnp.take(arrived, slot_of, axis=0)
    flat_blocks = blocks.reshape(request_count * block_len, enc_width)
    key_sum = jnp.dot(
        flat_blocks,
        lax.all_gather(w_key, "dp", axis=0, tiled=True),
        preferred_element_type=jnp.float32,
    )
    value_sum = jnp.dot(
        flat_blocks,
        lax.all_gather(w_value, "dp", axis=0, tiled=True),
        preferred_element_type=jnp.float32,
    )
    keys = key_sum.astype(jnp.bfloat16).reshape(stretch_count, KN * block_len, heads_here, HD)
    values = value_sum.astype(jnp.bfloat16).reshape(stretch_count, KN * block_len, heads_here, HD)
    positions = jnp.arange(block_len)
    key_valid = (positions[None, None, :] < nb_len[:, :, None]).reshape(
        stretch_count, KN * block_len
    )
    query_blocks = queries.reshape(stretch_count, CL, heads_here, HD)
    scores = (
        jnp.einsum("cqhd,ckhd->chqk", query_blocks, keys, preferred_element_type=jnp.float32)
        * score_scale
    )
    scores = jnp.where(key_valid[:, None, None, :], scores, -1e30)
    row_top = jnp.max(scores, axis=3, keepdims=True)
    weights_exp = jnp.exp(scores - row_top)
    prob_wide = weights_exp / jnp.sum(weights_exp, axis=3, keepdims=True)
    prob = prob_wide.astype(jnp.bfloat16)
    attended = jnp.einsum(
        "chqk,ckhd->cqhd", prob, values, preferred_element_type=jnp.float32
    ).astype(jnp.bfloat16)
    attended = attended.reshape(tok_rows, head_span)
    partial_out = jnp.dot(attended, output_full, preferred_element_type=jnp.float32)
    summed_out = lax.psum_scatter(
        partial_out.astype(jnp.bfloat16), "mp", scatter_dimension=1, tiled=True
    ).astype(jnp.float32)
    token_cols = lax.dynamic_slice_in_dim(wide_tokens, mp_place * width_share, width_share, 1)
    mixed = (token_cols + summed_out).astype(jnp.bfloat16)
    grad_attn = jnp.einsum(
        "td,sd->ts", grad_out, output_full, preferred_element_type=jnp.float32
    ).astype(jnp.bfloat16)
    grad_wout_part = jnp.einsum("ts,td->sd", attended, grad_out, preferred_element_type=jnp.float32)
    grad_blocks = grad_attn.reshape(stretch_count, CL, heads_here, HD)
    grad_prob = jnp.einsum(
        "cqhd,ckhd->chqk", grad_blocks, values, preferred_element_type=jnp.float32
    )
    grad_values = jnp.einsum(
        "chqk,cqhd->ckhd", prob, grad_blocks, preferred_element_type=jnp.float32
    ).astype(jnp.bfloat16)
    delta_rows = jnp.sum(prob_wide * grad_prob, axis=3, keepdims=True)
    grad_scores = (prob_wide * (grad_prob - delta_rows) * score_scale).astype(jnp.bfloat16)
    grad_queries = jnp.einsum(
        "chqk,ckhd->cqhd", grad_scores, keys, preferred_element_type=jnp.float32
    ).astype(jnp.bfloat16)
    grad_queries = grad_queries.reshape(tok_rows, head_span)
    grad_keys = jnp.einsum(
        "chqk,cqhd->ckhd", grad_scores, query_blocks, preferred_element_type=jnp.float32
    ).astype(jnp.bfloat16)
    grad_keys = grad_keys.reshape(request_count * block_len, head_span)
    grad_values = grad_values.reshape(request_count * block_len, head_span)
    grad_wq_part = jnp.einsum("td,ts->ds", normed, grad_queries, preferred_element_type=jnp.float32)
    grad_wk_part = jnp.einsum(
        "re,rs->es", flat_blocks, grad_keys, preferred_element_type=jnp.float32
    )
    grad_wv_part = jnp.einsum(
        "re,rs->es", flat_blocks, grad_values, preferred_element_type=jnp.float32
    )
    grad_query, grad_key, grad_value, grad_wout = (
        lax.psum_scatter(
            grad_wq_part.astype(jnp.bfloat16), "dp", scatter_dimension=0, tiled=True
        ).astype(jnp.float32),
        lax.psum_scatter(
            grad_wk_part.astype(jnp.bfloat16), "dp", scatter_dimension=0, tiled=True
        ).astype(jnp.float32),
        lax.psum_scatter(
            grad_wv_part.astype(jnp.bfloat16), "dp", scatter_dimension=0, tiled=True
        ).astype(jnp.float32),
        lax.psum_scatter(
            grad_wout_part.astype(jnp.bfloat16), "dp", scatter_dimension=1, tiled=True
        ).astype(jnp.float32),
    )
    grad_normed_part = jnp.einsum(
        "ts,ds->td", grad_queries, query_full, preferred_element_type=jnp.float32
    )
    out_cols = lax.dynamic_slice_in_dim(grad_out, mp_place * width_share, width_share, 1).astype(
        jnp.float32
    )
    normed_cols = lax.dynamic_slice_in_dim(normed_wide, mp_place * width_share, width_share, 1)
    grad_normed = lax.psum_scatter(
        grad_normed_part.astype(jnp.bfloat16), "mp", scatter_dimension=1, tiled=True
    ).astype(jnp.float32)
    stat_part = jnp.sum(grad_normed * normed_cols, axis=1, keepdims=True)
    stat_rows = lax.psum(stat_part, "mp") / width
    grad_here = inv_rms * (grad_normed - normed_cols * stat_rows)
    grad_tokens = (out_cols + grad_here).astype(jnp.bfloat16)
    return (mixed, grad_tokens, grad_query, grad_key, grad_value, grad_wout)


def solution(mesh):
    return jax.shard_map(
        on_device,
        mesh=mesh,
        in_specs=(
            P("dp", None),
            P("dp", None, None),
            P("dp", None),
            P("dp", None),
            P("dp", None),
            P("dp", "mp"),
            P("dp", "mp"),
            P("dp", "mp"),
            P("mp", "dp"),
            P("dp", None),
        ),
        out_specs=(
            P("dp", "mp"),
            P("dp", "mp"),
            P("dp", "mp"),
            P("dp", "mp"),
            P("dp", "mp"),
            P("mp", "dp"),
        ),
        check_vma=False,
    )
```

profile of v0, /device:TPU:0, one launch (start us, length us, event | category | flops | bytes accessed | tf_op | source)
XLA Modules:
  0.0 676.3 jit_solution(1701481415545263321)
XLA Ops:
  7.2 0.7 all-gather.9.cloned.1.call-update
  7.9 0.7 all-gather.5.cloned.1.call-update
  8.7 0.7 all-gather.7.cloned.1.call-update
  9.4 0.5 all-gather.11.cloned.1.call-update
  10.0 0.8 copy.90
  10.8 0.7 broadcast_add_fusion
  11.5 0.1 copy.91
  11.6 0.1 add.108
  11.6 0.2 convert_reduce_fusion
  11.8 0.1 select_reduce_fusion
  12.0 9.6 %all_to_all.11 = s32[8,1,3]{2,1,0:T(1,128)S(1)} all-to-all(s32[8,1,3]{2,1,0:T(1,128)S(1)} %bitcast.109), channel_id=1, replica_groups=mesh['dp'=8,'mp'=4] {'dp'}, dimensions={0} | all-to-all | bytes 192 | tf_op jit(solution)/shard_map/all_to_all | solution.py:40
  21.7 0.1 copy.95
  21.8 0.1 reshape.235
  21.9 0.1 copy.94
  22.0 6.5 gather_fusion
  28.5 5.7 broadcast_select_fusion
  34.2 4.8 all-to-all-start.1
  39.1 0.1 copy.96
  39.4 3.1 multiply_reduce_fusion
  42.5 67.1 %all-to-all-done.1 = bf16[8,3,128,896]{3,2,1,0:T(8,128)(2,1)} async-done(((bf16[8,3,128,896]{3,2,1,0:T(8,128)(2,1)}), bf16[8,3,128,896]{3,2,1,0:T(8,128)(2,1)}, u32[]{:S(2)}, u32[]{:S(2)}) %all-to-all-start.1) | async-done | bytes 5505056 | tf_op jit(solution)/shard_map/all_to_all | solution.py:43
  109.6 5.4 gather_fusion.1
  115.0 3.7 bitcast_select_fusion
  118.8 7.1 %convert_bitcast_fusion.2 = bf16[256,8,8,128]{3,1,2,0:T(8,128)(2,1)S(1)} fusion(bf16[2048,896]{1,0:T(8,128)(2,1)} %bitcast_select_fusion, bf16[896,1024]{1,0:T(8,128)(2,1)} %all-gather.9.cloned.1.call-done), kind=kOutput, calls=%fused_computation.23 | convolution fusion | flops 3760193536 | bytes 9699328 | tf_op jit(solution)/shard_map/dot_general | solution.py:47
  125.9 3.1 copy.111
  129.0 7.1 %convert_bitcast_fusion.3 = bf16[256,8,8,128]{3,1,2,0:T(8,128)(2,1)S(1)} fusion(bf16[2048,896]{1,0:T(8,128)(2,1)} %bitcast_select_fusion, bf16[896,1024]{1,0:T(8,128)(2,1)} %all-gather.5.cloned.1.call-done), kind=kOutput, calls=%fused_computation.25 | convolution fusion | flops 3760193536 | bytes 9699328 | tf_op jit(solution)/shard_map/dot_general | solution.py:52
  136.1 3.1 copy.112
  139.2 2.2 broadcast_select_fusion.1
  141.4 10.9 %all-gather.7.cloned.1.call-done = bf16[4096,1024]{1,0:T(8,128)(2,1)} async-done(((bf16[512,1024]{1,0:T(8,128)(2,1)}), bf16[4096,1024]{1,0:T(8,128)(2,1)}) %all-gather.7.cloned.1.call-update) | async-done | bytes 8388624 | tf_op jit(solution)/shard_map/all_gather | solution.py:28
  152.3 9.4 %fusion.60 = bf16[64,8,8,128]{3,1,2,0:T(8,128)(2,1)S(1)} fusion(bf16[4096,1024]{1,0:T(8,128)(2,1)} %all-gather.7.cloned.1.call-done, f32[512]{0:T(512)S(1)} %add_rsqrt_fusion, bf16[512,4096]{1,0:T(8,128)(2,1)} %param.10), kind=kOutput, calls=%fused_computation.60 | convolution fusion | flops 4301783040 | bytes 13633536 | tf_op jit(solution)/shard_map/dot_general | solution.py:30
  161.8 0.3 copy.110
  162.0 48.0 %all-gather.11.cloned.1.call-done = bf16[1024,4096]{1,0:T(8,128)(2,1)} async-done(((bf16[1024,512]{1,0:T(8,128)(2,1)}), bf16[1024,4096]{1,0:T(8,128)(2,1)}) %all-gather.11.cloned.1.call-update) | async-done | bytes 8388624 | tf_op jit(solution)/shard_map/all_gather | solution.py:29
  210.1 9.3 %fusion.59 = bf16[64,8,8,128]{3,1,2,0:T(8,128)(2,1)S(1)} fusion(bf16[512,4096]{1,0:T(8,128)(2,1)} %param.19, bf16[1024,4096]{1,0:T(8,128)(2,1)} %all-gather.11.cloned.1.call-done), kind=kOutput, calls=%fused_computation.59 | convolution fusion | flops 4295491584 | bytes 13631488 | tf_op jit(solution)/shard_map/td,sd->ts/dot_general | solution.py:83
  219.4 0.3 copy.114
  219.7 1.6 fusion.15
  221.2 3.2 fusion.85
  224.5 3.5 fusion.9
  228.0 30.5 %convert_bitcast_fusion.1 = bf16[8,256,8,128]{1,3,2,0:T(8,128)(2,1)} fusion(f32[8,8,64,256]{3,2,1,0:T(8,128)} %fusion.9, bf16[8,64,8,128]{3,2,1,0:T(8,128)(2,1)S(1)} %bitcast.100, f32[8,8,64,256]{3,2,1,0:T(8,128)} %get-tuple-element.9, f32[8,8,64]{2,1,0:T(8,128)S(1)} %get-tuple-element.8), kind=kOutput, calls=%fused_computation.17 | convolution fusion | flops 277876992 | bytes 13647872 | tf_op jit(solution)/shard_map/chqk,cqhd->ckhd/dot_general | solution.py:100
  258.5 6.7 copy.106
  265.2 8.5 %fusion.34 = bf16[896,1024]{1,0:T(8,128)(2,1)} fusion(bf16[2048,896]{1,0:T(8,128)(2,1)} %bitcast.103, bf16[256,8,8,128]{3,2,1,0:T(8,128)(2,1)} %bitcast.102), kind=kOutput, calls=%fused_computation.51 | convolution fusion | flops 3759013888 | bytes 9699328 | tf_op jit(solution)/shard_map/re,rs->es/dot_general | solution.py:106
  273.8 5.7 convert_bitcast_fusion
  279.5 6.9 %copy.108 = bf16[8,256,8,128]{3,2,1,0:T(8,128)(2,1)} copy(bf16[8,256,8,128]{1,3,2,0:T(8,128)(2,1)} %convert_bitcast_fusion) | data formatting | bytes 8388608 | tf_op jit(solution)/shard_map/convert_element_type | solution.py:93
  286.4 8.6 %fusion.37 = bf16[896,1024]{1,0:T(8,128)(2,1)} fusion(bf16[2048,896]{1,0:T(8,128)(2,1)} %bitcast.104, bf16[256,8,8,128]{3,2,1,0:T(8,128)(2,1)} %bitcast.101), kind=kOutput, calls=%fused_computation.52 | convolution fusion | flops 3759013888 | bytes 9699328 | tf_op jit(solution)/shard_map/re,rs->es/dot_general | solution.py:109
  295.0 28.1 %fusion.54 = bf16[8,64,8,128]{3,1,2,0:T(8,128)(2,1)S(1)} fusion(bf16[8,256,8,128]{3,2,1,0:T(8,128)(2,1)} %bitcast.95, f32[8,8,64,256]{3,2,1,0:T(8,128)} %fusion.9, f32[8,8,64,256]{3,2,1,0:T(8,128)} %get-tuple-element.9, f32[8,8,64]{2,1,0:T(8,128)S(1)} %get-tuple-element.8), kind=kOutput, calls=%fused_computation.58 | convolution fusion | flops 276304128 | bytes 13647872 | tf_op jit(solution)/shard_map/chqk,ckhd->cqhd/dot_general | solution.py:96
  323.1 0.7 copy.104
  323.8 10.0 %convolution_convert_fusion.2 = bf16[512,4096]{1,0:T(8,128)(2,1)} fusion(bf16[4096,1024]{1,0:T(8,128)(2,1)} %all-gather.7.cloned.1.call-done, bf16[64,8,8,128]{3,2,1,0:T(8,128)(2,1)S(1)} %bitcast.105), kind=kOutput, calls=%fused_computation.7 | convolution fusion | flops 4297064448 | bytes 13631488 | tf_op jit(solution)/shard_map/ts,ds->td/dot_general | solution.py:126
  333.8 4.5 fusion.51
  338.3 0.7 copy.100
  339.0 9.6 %convolution_convert_fusion.3 = bf16[512,4096]{1,0:T(8,128)(2,1)} fusion(bf16[1024,4096]{1,0:T(8,128)(2,1)} %all-gather.11.cloned.1.call-done, bf16[64,8,8,128]{3,2,1,0:T(8,128)(2,1)S(1)} %bitcast.107), kind=kOutput, calls=%fused_computation.8 | convolution fusion | flops 4297064448 | bytes 13631488 | tf_op jit(solution)/shard_map/dot_general | solution.py:77
  348.7 9.4 %convolution_convert_fusion.1 = bf16[4096,1024]{1,0:T(8,128)(2,1)} fusion(bf16[64,8,8,128]{3,2,1,0:T(8,128)(2,1)S(1)} %bitcast.106, f32[512]{0:T(512)S(1)} %add_rsqrt_fusion, bf16[512,4096]{1,0:T(8,128)(2,1)} %param.10), kind=kOutput, calls=%fused_computation.6 | convolution fusion | flops 4305453056 | bytes 13633536 | tf_op jit(solution)/shard_map/td,ts->ds/dot_general | solution.py:105
  358.1 9.0 %convolution_convert_fusion = bf16[1024,4096]{1,0:T(8,128)(2,1)} fusion(bf16[512,4096]{1,0:T(8,128)(2,1)} %param.19, bf16[64,8,8,128]{3,2,1,0:T(8,128)(2,1)S(1)} %bitcast.108), kind=kOutput, calls=%fused_computation.5 | convolution fusion | flops 4299161600 | bytes 13631488 | tf_op jit(solution)/shard_map/ts,td->sd/dot_general | solution.py:86
  367.2 6.5 convert_element_type.97
  373.6 6.7 broadcast_multiply_fusion
  380.3 1.8 convert_element_type.122
  382.1 1.7 convert_element_type.126
  383.8 52.5 %reduce-scatter.9.cloned.1.call-done = bf16[512,1024]{1,0:T(8,128)(2,1)} async-done(((bf16[512,4096]{1,0:T(8,128)(2,1)}), bf16[512,1024]{1,0:T(8,128)(2,1)}) %reduce-scatter.9.cloned.1.call-update) | async-done | bytes 1048592 | tf_op jit(solution)/shard_map/reduce_scatter | solution.py:133
  436.3 2.3 fusion.20
  438.6 11.1 %psum.7 = f32[512,1]{0,1:T(1,128)S(1)} all-reduce(f32[512,1]{0,1:T(1,128)S(1)} %bitcast.111), channel_id=1, replica_groups=mesh['dp'=8,'mp'=4] {'mp'}, use_global_device_ids=true, to_apply=%region_9.10 | all-reduce | flops 512 | bytes 4096 | tf_op jit(solution)/shard_map/psum | solution.py:137
  449.7 66.4 %reduce-scatter.7.cloned.1.call-done = bf16[512,1024]{1,0:T(8,128)(2,1)} async-done(((bf16[512,4096]{1,0:T(8,128)(2,1)}), bf16[512,1024]{1,0:T(8,128)(2,1)}) %reduce-scatter.7.cloned.1.call-update) | async-done | bytes 1048592 | tf_op jit(solution)/shard_map/reduce_scatter | solution.py:78
  516.1 3.2 add_convert_fusion
  519.4 3.3 fusion.23
  522.7 68.7 %reduce-scatter.11.cloned.1.call-done = bf16[512,1024]{1,0:T(8,128)(2,1)} async-done(((bf16[4096,1024]{1,0:T(8,128)(2,1)}), bf16[512,1024]{1,0:T(8,128)(2,1)}) %reduce-scatter.11.cloned.1.call-update) | async-done | bytes 1048592 | tf_op jit(solution)/shard_map/reduce_scatter | solution.py:113
  591.4 2.8 convert_element_type.118
  594.2 72.2 %reduce-scatter.17.cloned.1.call-done = bf16[1024,512]{1,0:T(8,128)(2,1)} async-done(((bf16[1024,4096]{1,0:T(8,128)(2,1)}), bf16[1024,512]{1,0:T(8,128)(2,1)}) %reduce-scatter.17.cloned.1.call-update) | async-done | bytes 1048592 | tf_op jit(solution)/shard_map/reduce_scatter | solution.py:122
  666.4 2.8 convert_element_type.128
  (50 shorter events, 1.1 us)
Async XLA Ops:
  7.2 111.6 %all-gather.9.cloned.1.call-start = ((), (), s32[]{:S(2)}) async-start(), calls=%async_computation.10 | async-start | bytes 2064384 | tf_op jit(solution)/shard_map/all_gather | solution.py:49
  7.9 121.1 %all-gather.5.cloned.1.call-start = ((), (), s32[]{:S(2)}) async-start(), calls=%async_computation.8 | async-start | bytes 2064384 | tf_op jit(solution)/shard_map/all_gather | solution.py:54
  8.6 143.7 %all-gather.7.cloned.1.call-start = ((), (), s32[]{:S(2)}) async-start(), calls=%async_computation.9 | async-start | bytes 9437184 | tf_op jit(solution)/shard_map/all_gather | solution.py:28
  9.4 200.7 %all-gather.11.cloned.1.call-start = ((), (), s32[]{:S(2)}) async-start(), calls=%async_computation.11 | async-start | bytes 9437184 | tf_op jit(solution)/shard_map/all_gather | solution.py:29
  34.2 4.9 copy-start.4
  34.2 75.4 %all-to-all-start.1 = ((bf16[8,3,128,896]{3,2,1,0:T(8,128)(2,1)}), bf16[8,3,128,896]{3,2,1,0:T(8,128)(2,1)}, u32[]{:S(2)}, u32[]{:S(2)}) async-start(bf16[8,3,128,896]{3,2,1,0:T(8,128)(2,1)} %broadcast_select_fusion), calls=%async_computation.1 | async-start | bytes 11010048 | tf_op jit(solution)/shard_map/all_to_all | solution.py:43
  39.0 3.4 copy-start.5
  39.0 341.3 %reduce-scatter.13.cloned.1.call-start = ((), (), s32[]{:S(2)}) async-start(), calls=%async_computation.15 | async-start | bytes 2064384 | tf_op jit(solution)/shard_map/reduce_scatter | solution.py:116
  136.1 3.1 copy-start
  210.0 9.6 %copy-start.2 = (bf16[256,8,8,128]{3,2,1,0:T(8,128)(2,1)S(1)}, bf16[256,8,8,128]{3,2,1,0:T(8,128)(2,1)}, u32[]{:S(2)}) copy-start(bf16[256,8,8,128]{3,2,1,0:T(8,128)(2,1)} %copy.111) | copy-start | bytes 12582916
  221.2 3.2 copy-start.1
  273.8 108.3 %reduce-scatter.15.cloned.1.call-start = ((), (), s32[]{:S(2)}) async-start(), calls=%async_computation.16 | async-start | bytes 2064384 | tf_op jit(solution)/shard_map/reduce_scatter | solution.py:119
  295.0 141.3 %reduce-scatter.9.cloned.1.call-start = ((), (), s32[]{:S(2)}) async-start(), calls=%async_computation.13 | async-start | bytes 5242880 | tf_op jit(solution)/shard_map/reduce_scatter | solution.py:133
  333.8 182.3 %reduce-scatter.7.cloned.1.call-start = ((), (), s32[]{:S(2)}) async-start(), calls=%async_computation.12 | async-start | bytes 5242880 | tf_op jit(solution)/shard_map/reduce_scatter | solution.py:78
  348.6 242.7 %reduce-scatter.11.cloned.1.call-start = ((), (), s32[]{:S(2)}) async-start(), calls=%async_computation.14 | async-start | bytes 9437184 | tf_op jit(solution)/shard_map/reduce_scatter | solution.py:113
  358.1 308.3 %reduce-scatter.17.cloned.1.call-start = ((), (), s32[]{:S(2)}) async-start(), calls=%async_computation.17 | async-start | bytes 9437184 | tf_op jit(solution)/shard_map/reduce_scatter | solution.py:122
  436.3 83.0 %copy-start.3 = (bf16[512,1024]{1,0:T(8,128)(2,1)S(1)}, bf16[512,1024]{1,0:T(8,128)(2,1)}, u32[]{:S(2)}) copy-start(bf16[512,1024]{1,0:T(8,128)(2,1)} %reduce-scatter.9.cloned.1.call-done) | copy-start | bytes 3145732
Sparse Core Ops, SparseCore 0:
  9.9 29.5 all-gather.8
  41.4 45.2 all-gather.4
  88.5 63.7 all-gather.6
  154.1 55.9 all-gather.10
  273.9 39.7 reduce-scatter.12
  317.5 39.7 reduce-scatter.14
  359.5 76.7 reduce-scatter.8
  438.7 77.3 reduce-scatter.6
  519.6 71.7 reduce-scatter.10
  595.1 71.2 reduce-scatter.16
where the time goes:
time: 681 us; the launch traced here: 676 us
  waiting for transfers between devices  388 us (57%)
  matrix products  162 us (24%)
  other arithmetic  50.2 us (7%)
  local copies, waits for them, and re-layouts  35.2 us (5%)
  blocking collectives  20.8 us (3%)
  between operations  14.6 us (2%)
    reduce_scatter x1, waiting for transfers between devices, on_device(): lax.psum_scatter(grad_wout_part.astype(jnp.bfloat16), 'dp', scatter_dimen...  72.2 us
    reduce_scatter x1, waiting for transfers between devices, on_device(): lax.psum_scatter(grad_wq_part.astype(jnp.bfloat16), 'dp', scatter_dimensi...  68.7 us
    all_to_all x1, waiting for transfers between devices, on_device(): lax.all_to_all(picked, 'dp', split_axis=0, concat_axis=0, tiled=True)  67.1 us
    reduce_scatter x1, waiting for transfers between devices, on_device(): lax.psum_scatter(partial_out.astype(jnp.bfloat16), 'mp', scatter_dimensio...  66.4 us
    reduce_scatter x1, waiting for transfers between devices, on_device(): lax.psum_scatter(grad_normed_part.astype(jnp.bfloat16), 'mp', scatter_dim...  52.5 us
    all_gather x1, waiting for transfers between devices, on_device(): output_full = lax.all_gather(w_out, 'dp', axis=1, tiled=True)  48 us
    dot_general x1, matrix products, on_device(): jnp.einsum('chqk,cqhd->ckhd', grad_scores, query_blocks, preferred_elemen...  30.5 us
    dot_general x1, matrix products, on_device(): jnp.einsum('chqk,ckhd->cqhd', grad_scores, keys, preferred_element_type=j...  28.1 us
  transfers between devices with their start and end apart: 11, of which 7 were waited for; matrix products, arithmetic and copies ran while one was open for 27% of the time, Pallas kernels for 0%

commit v1 on v0

v1 whole, which is shorter than its diff:
```python
import functools
import jax
import jax.numpy as jnp
from jax import lax
from jax.experimental import pallas as pl
from jax.experimental.pallas import tpu as pltpu
from jax.sharding import PartitionSpec as P

HD = 128
CL = 64
KN = 2
CAP = 3
MESH = pl.DeviceIdType.MESH
ANY = pl.BlockSpec(memory_space=pl.ANY)
SUB = 16


def places():
    me = lax.axis_index("dp")
    core, x, y = me % 2, (me // 2) % 2, me // 4
    sib = me + 1 - 2 * core
    dx, dy = 2 - 4 * x, 4 - 8 * y
    return me, sib, dx, dy


def greet(peers):
    barrier = pltpu.get_barrier_semaphore()
    for peer in peers:
        pl.semaphore_signal(barrier, inc=1, device_id={"dp": peer}, device_id_type=MESH)
    pl.semaphore_wait(barrier, len(peers))


def halves(rows):
    first = -(-(rows // 2) // SUB) * SUB
    return ((0, first), (first, rows - first))


def share_of(ref, axis, shape, index, start=0, size=None):
    rows, cols = shape
    size = rows if size is None else size
    if axis == 0:
        return ref.at[pl.ds(pl.multiple_of(index * rows + start, SUB), size), :]
    return ref.at[pl.ds(start, size), pl.ds(pl.multiple_of(index * cols, cols), cols)]


def gather_kernel(axes, shapes, *refs):
    count = len(axes)
    shards, fulls = refs[:count], refs[count : 2 * count]
    send, recv, local = refs[2 * count :]
    me, sib, dx, dy = places()
    greet((sib, me + dx, me + dy))
    started = []

    def place(a, owner, half):
        start, size = halves(shapes[a][0])[half]
        return share_of(fulls[a], axes[a], shapes[a], owner, start, size)

    def remote(a, source, owner, half, peer, slot):
        return pltpu.make_async_remote_copy(
            src_ref=source, dst_ref=place(a, owner, half), send_sem=send.at[a, slot],
            recv_sem=recv.at[a, slot], device_id={"dp": peer}, device_id_type=MESH)

    def push(a, source, owner, half, peer, slot):
        copy = remote(a, source, owner, half, peer, slot)
        copy.start()
        started.append(copy)

    def arrive(a, owner, half, slot):
        remote(a, place(a, owner, half), owner, half, sib, slot).wait_recv()

    own = []
    for a in range(count):
        parts = [shards[a].at[pl.ds(s, n), :] for s, n in halves(shapes[a][0])]
        push(a, parts[0], me, 0, me + dx, 0)
        push(a, parts[1], me, 1, me + dy, 3)
        push(a, parts[1], me, 1, me + dx, 1)
        push(a, parts[0], me, 0, me + dy, 2)
        for half in range(2):
            push(a, parts[half], me, half, sib, 4 + half)
            copy = pltpu.make_async_copy(parts[half], place(a, me, half), local.at[a, half])
            copy.start()
            own.append(copy)
    for a in range(count):
        near_x, near_y = me + dx, me + dy
        arrive(a, near_x, 0, 0)
        push(a, place(a, near_x, 0), near_x, 0, me + dy, 6)
        arrive(a, near_y, 1, 3)
        push(a, place(a, near_y, 1), near_y, 1, me + dx, 7)
        push(a, place(a, near_x, 0), near_x, 0, sib, 8)
        push(a, place(a, near_y, 1), near_y, 1, sib, 11)
        arrive(a, near_x, 1, 1)
        push(a, place(a, near_x, 1), near_x, 1, sib, 9)
        arrive(a, near_y, 0, 2)
        push(a, place(a, near_y, 0), near_y, 0, sib, 10)
    for a in range(count):
        far = me + dx + dy
        for half in range(2):
            arrive(a, far, half, 6 + half)
            push(a, place(a, far, half), far, half, sib, 12 + half)
    for a in range(count):
        for half in range(2):
            arrive(a, sib, half, 4 + half)
            arrive(a, sib + dx, half, 8 + half)
            arrive(a, sib + dy, half, 10 + half)
            arrive(a, sib + dx + dy, half, 12 + half)
    for copy in own:
        copy.wait()
    for copy in started:
        copy.wait_send()


def gather_all(shards, axes):
    dp_count = lax.axis_size("dp")
    if dp_count != 8:
        return [lax.all_gather(s, "dp", axis=a, tiled=True) for s, a in zip(shards, axes)]
    shapes = [s.shape for s in shards]
    outs = [jax.ShapeDtypeStruct((r * dp_count, c) if a == 0 else (r, c * dp_count), s.dtype)
            for s, a, (r, c) in zip(shards, axes, shapes)]
    count = len(shards)
    return pl.pallas_call(
        functools.partial(gather_kernel, axes, shapes),
        out_shape=outs,
        in_specs=[ANY] * count,
        out_specs=[ANY] * count,
        scratch_shapes=[pltpu.SemaphoreType.DMA((count, 14)), pltpu.SemaphoreType.DMA((count, 14)),
                        pltpu.SemaphoreType.DMA((count, 2))],
        compiler_params=pltpu.CompilerParams(collective_id=0, has_side_effects=True),
        name="gather_weights",
    )(*shards)


def scatter_kernel(axes, shapes, *refs):
    count = len(axes)
    parts, outs = refs[:count], refs[count : 2 * count]
    bufs = refs[2 * count : 6 * count]
    send, recv, local = refs[6 * count :]
    mine, cross = bufs[:count], bufs[count : 2 * count]
    via_x, via_y = bufs[2 * count : 3 * count], bufs[3 * count :]
    me, sib, dx, dy = places()
    moves = (0, dx, dy, dx + dy)
    near_x, near_y = me + dx, me + dy
    greet((sib, near_x, near_y))
    started, loads, crossings = [], {}, {}

    def push(a, source, target, peer, slot):
        copy = pltpu.make_async_remote_copy(
            src_ref=source, dst_ref=target, send_sem=send.at[a, slot],
            recv_sem=recv.at[a, slot], device_id={"dp": peer}, device_id_type=MESH)
        copy.start()
        started.append(copy)
        return copy

    def add(a, target, other, start, size):
        def step(i, _):
            rows = pl.ds(pl.multiple_of(start + i * SUB, SUB), SUB)
            target[rows, :] = (target[rows, :].astype(jnp.float32)
                               + other[rows, :].astype(jnp.float32)).astype(target.dtype)
            return 0
        lax.fori_loop(0, size // SUB, step, 0)

    for a in range(count):
        for r in (3, 1, 2, 0):
            crossings[a, r] = push(a, share_of(parts[a], axes[a], shapes[a], sib + moves[r]),
                                   cross[a].at[r], sib, r)
            load = pltpu.make_async_copy(share_of(parts[a], axes[a], shapes[a], me + moves[r]),
                                         mine[a].at[r], local.at[a, r])
            load.start()
            loads[a, r] = load
    hops = {}
    for a in range(count):
        rows = shapes[a][0]
        (a0, an), (b0, bn) = halves(rows)
        top, low = pl.ds(a0, an), pl.ds(b0, bn)
        for r in (3, 1, 2, 0):
            loads[a, r].wait()
            crossings[a, r].wait_recv()
            add(a, mine[a].at[r], cross[a].at[r], 0, rows)
            if r in (3, 1):
                k = r // 2
                hops[a, "x", k] = push(a, mine[a].at[r, top], via_x[a].at[k, top], near_x, 4 + k)
            if r in (3, 2):
                k = r - 2
                hops[a, "y", k] = push(a, mine[a].at[r, low], via_y[a].at[k, low], near_y, 6 + k)
    for a in range(count):
        (a0, an), (b0, bn) = halves(shapes[a][0])
        top, low = pl.ds(a0, an), pl.ds(b0, bn)
        hops[a, "x", 1].wait_recv()
        add(a, mine[a].at[2], via_x[a].at[1], a0, an)
        hops[a, "y", 2] = push(a, mine[a].at[2, top], via_y[a].at[0, top], near_y, 8)
        hops[a, "y", 1].wait_recv()
        add(a, mine[a].at[1], via_y[a].at[1], b0, bn)
        hops[a, "x", 2] = push(a, mine[a].at[1, low], via_x[a].at[0, low], near_x, 9)
    for a in range(count):
        for k in (0, 2):
            hops[a, "x", k].wait_recv()
            hops[a, "y", k].wait_recv()

        def finish(i, _, a=a):
            rows = pl.ds(pl.multiple_of(i * SUB, SUB), SUB)
            outs[a][rows, :] = (mine[a][0, rows, :].astype(jnp.float32)
                                + via_x[a][0, rows, :].astype(jnp.float32)
                                + via_y[a][0, rows, :].astype(jnp.float32))
            return 0
        lax.fori_loop(0, shapes[a][0] // SUB, finish, 0)
    for copy in started:
        copy.wait_send()


def scatter_all(parts, axes):
    dp_count = lax.axis_size("dp")
    if dp_count != 8:
        return [lax.psum_scatter(p, "dp", scatter_dimension=a, tiled=True).astype(jnp.float32)
                for p, a in zip(parts, axes)]
    shapes = [(p.shape[0] // dp_count, p.shape[1]) if a == 0 else (p.shape[0], p.shape[1] // dp_count)
              for p, a in zip(parts, axes)]
    count = len(parts)
    four = [pltpu.VMEM((4,) + s, jnp.bfloat16) for s in shapes]
    two = [pltpu.VMEM((2,) + s, jnp.bfloat16) for s in shapes]
    return pl.pallas_call(
        functools.partial(scatter_kernel, axes, shapes),
        out_shape=[jax.ShapeDtypeStruct(s, jnp.float32) for s in shapes],
        in_specs=[ANY] * count,
        out_specs=[pl.BlockSpec(memory_space=pltpu.VMEM)] * count,
        scratch_shapes=four + four + two + two
        + [pltpu.SemaphoreType.DMA((count, 10)), pltpu.SemaphoreType.DMA((count, 10)),
           pltpu.SemaphoreType.DMA((count, 4))],
        compiler_params=pltpu.CompilerParams(
            collective_id=1, has_side_effects=True, vmem_limit_bytes=56 * 2**20),
        name="scatter_gradients",
    )(*parts)


def pick_kernel(count, span, ids, source, out, sems):
    copies = []
    for i in range(count):
        row = source.at[ids[i], pl.ds(pl.multiple_of(ids[count] * span, SUB), span)]
        copy = pltpu.make_async_copy(row, out.at[i], sems.at[i])
        copy.start()
        copies.append(copy)
    for copy in copies:
        copy.wait()


def pick(source, ids, part, span):
    count = ids.shape[0]
    table = jnp.concatenate([ids, jnp.reshape(part, (1,))]).astype(jnp.int32)
    return pl.pallas_call(
        functools.partial(pick_kernel, count, span),
        out_shape=jax.ShapeDtypeStruct((count, span, source.shape[2]), source.dtype),
        in_specs=[pl.BlockSpec(memory_space=pltpu.SMEM), ANY],
        out_specs=ANY,
        scratch_shapes=[pltpu.SemaphoreType.DMA((count,))],
        name="pick_blocks",
    )(table, source)


def attend_kernel(heads, block_len, lens, q_ref, k_ref, v_ref, g_ref, att_ref, gq_ref, gk_ref, gv_ref):
    stretch = pl.program_id(0)
    scale = HD ** (-0.5)
    rows, span = q_ref.shape[0], k_ref.shape[0]
    at = lax.broadcasted_iota(jnp.int32, (rows, span), 1)
    valid = at < lens[stretch, 0]
    for j in range(1, KN):
        valid |= (at >= j * block_len) & (at < j * block_len + lens[stretch, j])

    def dot(left, right, sides):
        return lax.dot_general(left, right, (sides, ((), ())), preferred_element_type=jnp.float32)

    for h in range(heads):
        cols = slice(h * HD, (h + 1) * HD)
        q, k, v, g = q_ref[:, cols], k_ref[:, cols], v_ref[:, cols], g_ref[:, cols]
        scores = jnp.where(valid, dot(q, k, ((1,), (1,))) * scale, -1e30)
        expd = jnp.exp(scores - jnp.max(scores, axis=1, keepdims=True))
        wide = expd / jnp.sum(expd, axis=1, keepdims=True)
        prob = wide.astype(jnp.bfloat16)
        att_ref[:, cols] = dot(prob, v, ((1,), (0,))).astype(jnp.bfloat16)
        grad_prob = dot(g, v, ((1,), (1,)))
        gv_ref[:, cols] = dot(prob, g, ((0,), (0,))).astype(jnp.bfloat16)
        delta = jnp.sum(wide * grad_prob, axis=1, keepdims=True)
        grad_scores = (wide * (grad_prob - delta) * scale).astype(jnp.bfloat16)
        gq_ref[:, cols] = dot(grad_scores, k, ((1,), (0,))).astype(jnp.bfloat16)
        gk_ref[:, cols] = dot(grad_scores, q, ((0,), (0,))).astype(jnp.bfloat16)


def attend(nb_len, queries, keys, values, grads, block_len):
    stretches, width = nb_len.shape[0], queries.shape[1]
    small = pl.BlockSpec((CL, width), lambda c, lens: (c, 0))
    large = pl.BlockSpec((KN * block_len, width), lambda c, lens: (c, 0))
    like = lambda a: jax.ShapeDtypeStruct(a.shape, jnp.bfloat16)
    return pl.pallas_call(
        functools.partial(attend_kernel, width // HD, block_len),
        out_shape=[like(queries), like(queries), like(keys), like(values)],
        grid_spec=pltpu.PrefetchScalarGridSpec(
            num_scalar_prefetch=1, grid=(stretches,),
            in_specs=[small, large, large, small],
            out_specs=[small, small, large, large]),
        compiler_params=pltpu.CompilerParams(vmem_limit_bytes=32 * 2**20),
        name="attend",
    )(nb_len, queries, keys, values, grads)


def on_device(tokens, cache, nb_row, nb_owner, nb_len, w_query, w_key, w_value, w_out, grad_out):
    dp_count = lax.axis_size("dp")
    mp_count = lax.axis_size("mp")
    mp_place = lax.axis_index("mp")
    tok_rows, width = tokens.shape
    head_span = w_query.shape[1]
    heads_here = head_span // HD
    stretch_count = nb_row.shape[0]
    request_count = stretch_count * KN
    cache_rows, block_len, enc_width = cache.shape
    width_share = width // mp_count
    wide_tokens = tokens.astype(jnp.float32)
    inv_rms = lax.rsqrt(jnp.mean(wide_tokens * wide_tokens, axis=1, keepdims=True) + 1e-06)
    normed_wide = wide_tokens * inv_rms
    normed = normed_wide.astype(jnp.bfloat16)
    owners = nb_owner.reshape(-1)
    wanted = nb_row.reshape(-1)
    req_order = jnp.arange(request_count)
    earlier = (owners[:, None] == owners[None, :]) & (req_order[None, :] < req_order[:, None])
    rank_seen = jnp.sum(earlier.astype(jnp.int32), axis=1)
    slot_of = owners * CAP + rank_seen
    slot_hits = (slot_of[:, None] == jnp.arange(dp_count * CAP)[None, :]).astype(jnp.int32)
    asked_ids = (jnp.sum(slot_hits * (wanted[:, None] + 1), axis=0) - 1).reshape(dp_count, CAP)
    picked_rows = jnp.clip(
        lax.all_to_all(asked_ids, "dp", split_axis=0, concat_axis=0, tiled=True), 0, cache_rows - 1
    )
    span = block_len // mp_count
    picked = pick(cache, picked_rows.reshape(-1), mp_place, span)
    picked = picked.reshape(dp_count, CAP, span, enc_width)
    arrived = lax.all_to_all(picked, "dp", split_axis=0, concat_axis=0, tiled=True)
    arrived = arrived.reshape(dp_count * CAP, span, enc_width)
    chosen = pick(arrived, slot_of, jnp.int32(0), span)
    blocks = lax.all_gather(chosen, "mp", axis=1, tiled=True)
    flat_blocks = blocks.reshape(request_count * block_len, enc_width)
    query_full, output_full, key_full, value_full = gather_all(
        (w_query, w_out, w_key, w_value), (0, 1, 0, 0)
    )
    queries = jnp.dot(normed, query_full, preferred_element_type=jnp.float32).astype(jnp.bfloat16)
    grad_attn = jnp.einsum(
        "td,sd->ts", grad_out, output_full, preferred_element_type=jnp.float32
    ).astype(jnp.bfloat16)
    keys = jnp.dot(flat_blocks, key_full, preferred_element_type=jnp.float32).astype(jnp.bfloat16)
    values = jnp.dot(flat_blocks, value_full, preferred_element_type=jnp.float32).astype(jnp.bfloat16)
    attended, grad_queries, grad_keys, grad_values = attend(
        nb_len, queries, keys, values, grad_attn, block_len
    )
    partial_out = jnp.dot(attended, output_full, preferred_element_type=jnp.float32)
    summed_out = lax.psum_scatter(
        partial_out.astype(jnp.bfloat16), "mp", scatter_dimension=1, tiled=True
    ).astype(jnp.float32)
    token_cols = lax.dynamic_slice_in_dim(tokens, mp_place * width_share, width_share, 1).astype(
        jnp.float32
    )
    mixed = (token_cols + summed_out).astype(jnp.bfloat16)
    grad_wout_part = jnp.einsum("ts,td->sd", attended, grad_out, preferred_element_type=jnp.float32)
    grad_wq_part = jnp.einsum("td,ts->ds", normed, grad_queries, preferred_element_type=jnp.float32)
    grad_wk_part = jnp.einsum(
        "re,rs->es", flat_blocks, grad_keys, preferred_element_type=jnp.float32
    )
    grad_wv_part = jnp.einsum(
        "re,rs->es", flat_blocks, grad_values, preferred_element_type=jnp.float32
    )
    grad_query, grad_wout, grad_key, grad_value = scatter_all(
        [p.astype(jnp.bfloat16) for p in (grad_wq_part, grad_wout_part, grad_wk_part, grad_wv_part)],
        (0, 1, 0, 0),
    )
    grad_normed_part = jnp.einsum(
        "ts,ds->td", grad_queries, query_full, preferred_element_type=jnp.float32
    )
    out_cols = lax.dynamic_slice_in_dim(grad_out, mp_place * width_share, width_share, 1).astype(
        jnp.float32
    )
    normed_cols = token_cols * inv_rms
    grad_normed = lax.psum_scatter(
        grad_normed_part.astype(jnp.bfloat16), "mp", scatter_dimension=1, tiled=True
    ).astype(jnp.float32)
    stat_part = jnp.sum(grad_normed * normed_cols, axis=1, keepdims=True)
    stat_rows = lax.psum(stat_part, "mp") / width
    grad_here = inv_rms * (grad_normed - normed_cols * stat_rows)
    grad_tokens = (out_cols + grad_here).astype(jnp.bfloat16)
    return (mixed, grad_tokens, grad_query, grad_key, grad_value, grad_wout)


def solution(mesh):
    return jax.shard_map(
        on_device,
        mesh=mesh,
        in_specs=(
            P("dp", None),
            P("dp", None, None),
            P("dp", None),
            P("dp", None),
            P("dp", None),
            P("dp", "mp"),
            P("dp", "mp"),
            P("dp", "mp"),
            P("mp", "dp"),
            P("dp", None),
        ),
        out_specs=(
            P("dp", "mp"),
            P("dp", "mp"),
            P("dp", "mp"),
            P("dp", "mp"),
            P("dp", "mp"),
            P("mp", "dp"),
        ),
        check_vma=False,
    )
```

time: 681 us -> 447 us (0.66)
  waiting for transfers between devices: 388 us -> 35 us
  Pallas kernels: 0 us -> 284 us
  matrix products: 162 us -> 67 us
  other arithmetic: 50.2 us -> 12 us
  local copies, waits for them, and re-layouts: 35.2 us -> 13.5 us
  blocking collectives: 20.8 us -> 12.6 us
    pallas_call x0 -> x5, Pallas kernels: none -> 284 us  [the longest x1 92.3 us: scatter_all(): pl.pallas_call(functools.partial(scatter_kernel, axes, shapes), out_shape...]
    reduce_scatter x4 -> x0, waiting for transfers between devices: 141 us -> none  [the longest x1 72.2 us: on_device(): lax.psum_scatter(grad_wout_part.astype(jnp.bfloat16), 'dp', scatter_dimen...]
    dot_general x8 -> x2, matrix products: 88.1 us -> 12 us  [the longest x1 7.28 us: on_device(): jnp.dot(flat_blocks, key_full, preferred_element_type=jnp.float32)]
    all_gather x4 -> x1, waiting for transfers between devices: 58.9 us -> 0.02 us  [on_device(): blocks = lax.all_gather(chosen, 'mp', axis=1, tiled=True)]
    reduce_scatter x1, waiting for transfers between devices: 66.4 us -> 12.1 us  [on_device(): lax.psum_scatter(partial_out.astype(jnp.bfloat16), 'mp', scatter_dimensio...]
    reduce_scatter x1, waiting for transfers between devices: 52.5 us -> 0.02 us  [on_device(): lax.psum_scatter(grad_normed_part.astype(jnp.bfloat16), 'mp', scatter_dim...]
    all_to_all x1, waiting for transfers between devices: 67.1 us -> 18.2 us  [on_device(): lax.all_to_all(picked, 'dp', split_axis=0, concat_axis=0, tiled=True)]
    convert_element_type x6 -> x0, other arithmetic: 18.8 us -> none  [the longest x4 9.13 us: on_device(): grad_query, grad_key, grad_value, grad_wout = (lax.psum_scatter(grad_wq_p...]
  transfers between devices with their start and end apart: 11 -> 5, of which waited for: 7 -> 3; matrix products, arithmetic and copies ran while one was open for 27% -> 12% of each run, Pallas kernels for 0% -> 40%
where the time goes in v1:
time: 447 us
  Pallas kernels  284 us (64%)
  matrix products  67 us (15%)
  waiting for transfers between devices  35 us (8%)
  between operations  14 us (3%)
  local copies, waits for them, and re-layouts  13.5 us (3%)
  blocking collectives  12.6 us (3%)
  other arithmetic  12 us (3%)
  starting transfers between devices  8.88 us (2%)
    pallas_call x1, Pallas kernels, scatter_all(): pl.pallas_call(functools.partial(scatter_kernel, axes, shapes), out_shape...  92.3 us
    pallas_call x1, Pallas kernels, gather_all(): pl.pallas_call(functools.partial(gather_kernel, axes, shapes), out_shape=...  87.6 us
    pallas_call x2, Pallas kernels, pick(): pl.pallas_call(functools.partial(pick_kernel, count, span), out_shape=jax...  73.4 us
    pallas_call x1, Pallas kernels, attend(): pl.pallas_call(functools.partial(attend_kernel, width // HD, block_len),...  30.3 us
    all_to_all x1, waiting for transfers between devices, on_device(): lax.all_to_all(picked, 'dp', split_axis=0, concat_axis=0, tiled=True)  18.2 us
    psum x1, blocking collectives, on_device(): stat_rows = lax.psum(stat_part, 'mp') / width  12.6 us
    unnamed x50, local copies, waits for them, and re-layouts  12.5 us
    reduce_scatter x1, waiting for transfers between devices, on_device(): lax.psum_scatter(partial_out.astype(jnp.bfloat16), 'mp', scatter_dimensio...  12.1 us
  transfers between devices with their start and end apart: 5, of which 3 were waited for; matrix products, arithmetic and copies ran while one was open for 12% of the time, Pallas kernels for 40%

profile of v1, /device:TPU:0, one launch (start us, length us, event | category | flops | bytes accessed | tf_op | source)
XLA Modules:
  0.0 446.5 jit_solution(16008923323343135190)
XLA Ops:
  7.2 0.7 broadcast_add_fusion
  7.8 0.1 copy.30
  7.9 0.1 add.60
  8.0 0.8 copy.29
  8.8 0.1 reshape.75
  8.9 0.2 convert_reduce_fusion
  9.0 0.1 select_reduce_fusion
  9.1 0.7 sub.9
  9.8 5.2 %all-to-all-start = ((s32[8,1,3]{2,1,0:T(1,128)}), s32[8,1,3]{2,1,0:T(1,128)S(1)}, u32[]{:S(2)}, u32[]{:S(2)}) async-start(s32[8,1,3]{2,1,0:T(1,128)} %bitcast), calls=%async_computation | async-start | bytes 8192 | tf_op jit(solution)/shard_map/all_to_all | solution.py:326
  15.0 4.6 %all-to-all-done = s32[8,1,3]{2,1,0:T(1,128)S(1)} async-done(((s32[8,1,3]{2,1,0:T(1,128)}), s32[8,1,3]{2,1,0:T(1,128)S(1)}, u32[]{:S(2)}, u32[]{:S(2)}) %all-to-all-start) | async-done | bytes 128 | tf_op jit(solution)/shard_map/all_to_all | solution.py:326
  19.6 0.1 min.12
  19.7 0.6 pad_add_fusion.1.ids
  20.3 43.7 %pick_blocks.2 = bf16[24,32,896]{2,1,0:T(8,128)(2,1)} custom-call(s32[25]{0:T(128)} %pad_add_fusion.1.ids, bf16[24,128,896]{2,1,0:T(8,128)(2,1)} %source.1), custom_call_target="tpu_custom_call" | custom-call | tf_op jit(solution)/shard_map/pick_blocks/pallas_call | solution.py:247
  64.0 0.0 copy-start.14
  64.0 3.6 all-to-all-start.1
  67.6 0.0 all-gather.2.cloned.1.call-start
  67.6 0.6 pad_add_fusion.ids
  68.2 18.2 %all-to-all-done.1 = bf16[8,3,32,896]{3,2,1,0:T(8,128)(2,1)S(1)} async-done(((bf16[8,3,32,896]{3,2,1,0:T(8,128)(2,1)}), bf16[8,3,32,896]{3,2,1,0:T(8,128)(2,1)S(1)}, u32[]{:S(2)}, u32[]{:S(2)}) %all-to-all-start.1) | async-done | bytes 1376288 | tf_op jit(solution)/shard_map/all_to_all | solution.py:331
  86.4 1.1 copy-done.7
  87.5 29.7 %pick_blocks.3 = bf16[16,32,896]{2,1,0:T(8,128)(2,1)} custom-call(s32[17]{0:T(128)} %pad_add_fusion.ids, bf16[24,32,896]{2,1,0:T(8,128)(2,1)} %bitcast.27), custom_call_target="tpu_custom_call" | custom-call | tf_op jit(solution)/shard_map/pick_blocks/pallas_call | solution.py:247
  117.2 0.0 all-gather.2.cloned.1.call-update
  117.2 0.0 reduce-scatter.5.cloned.1.call-start
  117.3 0.0 copy-done.14
  117.3 0.1 copy.33.lens
  117.4 87.6 %gather_weights.1 = (bf16[4096,1024]{1,0:T(8,128)(2,1)}, bf16[1024,4096]{1,0:T(8,128)(2,1)}, bf16[896,1024]{1,0:T(8,128)(2,1)}, bf16[896,1024]{1,0:T(8,128)(2,1)}) custom-call(bf16[512,1024]{1,0:T(8,128)(2,1)} %refs_0_.1, bf16[1024,512]{1,0:T(8,128)(2,1)} %refs_1_.1, bf16[112,1024]{1,0:T(8,128)(2,1)} %refs_2_.1, bf16[112,1024]{1,0:T(8,128)(2,1)} %refs_3_.1), custom_call_target="tpu_custom_call" | custom-call | tf_op jit(solution)/shard_map/gather_weights/pallas_call | solution.py:120
  205.0 0.0 copy-start.12
  205.0 0.0 slice-start
  205.0 3.2 fusion
  208.3 0.2 copy-done.12
  208.4 7.4 %fusion.14.g_ref = bf16[512,1024]{1,0:T(8,128)(2,1)S(1)} fusion(bf16[1024,4096]{1,0:T(8,128)(2,1)} %get-tuple-element.21, bf16[512,4096]{1,0:T(8,128)(2,1)S(1)} %copy-done.12), kind=kOutput, calls=%fused_computation.25 | convolution fusion | flops 4295491584 | bytes 13631488 | tf_op jit(solution)/shard_map/td,sd->ts/dot_general | solution.py:340
  215.9 0.0 slice-done
  215.9 4.6 %fusion.11.q_ref = bf16[512,1024]{1,0:T(8,128)(2,1)S(1)} fusion(bf16[4096,1024]{1,0:T(8,128)(2,1)S(1)} %bitcast.32, bf16[512,4096]{1,0:T(8,128)(2,1)S(1)} %copy-done.5, f32[512]{0:T(512)S(1)} %add_rsqrt_fusion), kind=kOutput, calls=%fused_computation.23 | convolution fusion | flops 4301783040 | bytes 13633536 | tf_op jit(solution)/shard_map/dot_general | solution.py:339
  220.5 0.0 all-gather.2.cloned.1.call-done
  220.5 0.0 slice-start.2
  220.5 7.3 %convolution_convert_fusion.5.k_ref = bf16[2048,1024]{1,0:T(8,128)(2,1)S(1)} fusion(bf16[2048,896]{1,0:T(8,128)(2,1)} %bitcast.35, bf16[896,1024]{1,0:T(8,128)(2,1)} %get-tuple-element.19), kind=kOutput, calls=%fused_computation.9 | convolution fusion | flops 3760193536 | bytes 9699328 | tf_op jit(solution)/shard_map/dot_general | solution.py:343
  227.8 0.0 slice-start.3
  227.8 4.7 %convolution_convert_fusion.4.v_ref = bf16[2048,1024]{1,0:T(8,128)(2,1)S(1)} fusion(bf16[2048,896]{1,0:T(8,128)(2,1)S(1)} %bitcast.37, bf16[896,1024]{1,0:T(8,128)(2,1)S(1)} %copy-done.17), kind=kOutput, calls=%fused_computation.8 | convolution fusion | flops 3760193536 | bytes 9699328 | tf_op jit(solution)/shard_map/dot_general | solution.py:344
  232.6 30.3 %attend.1 = (bf16[512,1024]{1,0:T(8,128)(2,1)S(1)}, bf16[512,1024]{1,0:T(8,128)(2,1)S(1)}, bf16[2048,1024]{1,0:T(8,128)(2,1)S(1)}, bf16[2048,1024]{1,0:T(8,128)(2,1)S(1)}) custom-call(s32[8,2]{1,0:T(8,128)S(1)} %copy.33.lens, bf16[512,1024]{1,0:T(8,128)(2,1)S(1)} %fusion.11.q_ref, bf16[2048,1024]{1,0:T(8,128)(2,1)S(1)} %convolution_convert_fusion.5.k_ref, ...), custom_call_target="tpu_custom_call" | custom-call | tf_op jit(solution)/shard_map/attend/pallas_call | solution.py:290
  262.9 2.0 copy-done
  264.9 2.1 copy-done.2
  267.0 1.0 copy-done.3
  268.0 6.1 %convolution_convert_fusion.2 = bf16[512,4096]{1,0:T(8,128)(2,1)} fusion(bf16[512,1024]{1,0:T(8,128)(2,1)S(1)} %get-tuple-element.23, bf16[4096,1024]{1,0:T(8,128)(2,1)S(1)} %bitcast.34), kind=kOutput, calls=%fused_computation.6 | convolution fusion | flops 4297064448 | bytes 13631488 | tf_op jit(solution)/shard_map/ts,ds->td/dot_general | solution.py:368
  274.1 0.0 reduce-scatter.5.cloned.1.call-update
  274.1 0.0 reduce-scatter.3.cloned.1.call-start
  274.1 1.1 copy-done.4
  275.3 9.5 %convolution_convert_fusion.3 = bf16[512,4096]{1,0:T(8,128)(2,1)} fusion(bf16[512,1024]{1,0:T(8,128)(2,1)S(1)} %copy-done.4, bf16[1024,4096]{1,0:T(8,128)(2,1)} %get-tuple-element.21), kind=kOutput, calls=%fused_computation.7 | convolution fusion | flops 4297064448 | bytes 13631488 | tf_op jit(solution)/shard_map/dot_general | solution.py:348
  284.8 0.0 reduce-scatter.3.cloned.1.call-update
  284.8 0.0 copy-start.1
  284.8 0.0 copy-start.16
  284.8 8.7 %convolution_convert_fusion.7.refs_2_ = bf16[896,1024]{1,0:T(8,128)(2,1)} fusion(bf16[2048,896]{1,0:T(8,128)(2,1)} %bitcast.36, bf16[2048,1024]{1,0:T(8,128)(2,1)} %copy-done.2), kind=kOutput, calls=%fused_computation.21 | convolution fusion | flops 3759013888 | bytes 9699328 | tf_op jit(solution)/shard_map/re,rs->es/dot_general | solution.py:358
  293.5 5.1 %convolution_convert_fusion.6.refs_3_ = bf16[896,1024]{1,0:T(8,128)(2,1)} fusion(bf16[2048,896]{1,0:T(8,128)(2,1)S(1)} %bitcast.38, bf16[2048,1024]{1,0:T(8,128)(2,1)S(1)} %copy-done.1), kind=kOutput, calls=%fused_computation.20 | convolution fusion | flops 3759013888 | bytes 9699328 | tf_op jit(solution)/shard_map/re,rs->es/dot_general | solution.py:361
  298.6 6.7 %convolution_convert_fusion.refs_1_ = bf16[1024,4096]{1,0:T(8,128)(2,1)} fusion(bf16[512,1024]{1,0:T(8,128)(2,1)S(1)} %copy-done.4, bf16[512,4096]{1,0:T(8,128)(2,1)S(1)} %copy-done.13), kind=kOutput, calls=%fused_computation.4 | convolution fusion | flops 4299161600 | bytes 13631488 | tf_op jit(solution)/shard_map/ts,td->sd/dot_general | solution.py:356
  305.3 6.9 %convolution_convert_fusion.1.refs_0_ = bf16[4096,1024]{1,0:T(8,128)(2,1)} fusion(bf16[512,1024]{1,0:T(8,128)(2,1)S(1)} %get-tuple-element.23, bf16[512,4096]{1,0:T(8,128)(2,1)S(1)} %copy-done.6, f32[512]{0:T(512)S(1)} %add_rsqrt_fusion), kind=kOutput, calls=%fused_computation.5 | convolution fusion | flops 4305453056 | bytes 13633536 | tf_op jit(solution)/shard_map/td,ts->ds/dot_general | solution.py:357
  312.3 92.3 %scatter_gradients.1 = (f32[512,1024]{1,0:T(8,128)}, f32[1024,512]{1,0:T(8,128)}, f32[112,1024]{1,0:T(8,128)}, f32[112,1024]{1,0:T(8,128)}) custom-call(bf16[4096,1024]{1,0:T(8,128)(2,1)} %convolution_convert_fusion.1.refs_0_, bf16[1024,4096]{1,0:T(8,128)(2,1)} %convolution_convert_fusion.refs_1_, bf16[896,1024]{1,0:T(8,128)(2,1)} %convolution_convert_fusion.7.refs_2_, ...), custom_call_target="tpu_custom_call" | custom-call | tf_op jit(solution)/shard_map/scatter_gradients/pallas_call | solution.py:219
  404.5 0.0 reduce-scatter.5.cloned.1.call-done
  404.6 2.2 fusion.4
  406.8 12.6 %psum.7 = f32[512,1]{0,1:T(1,128)S(1)} all-reduce(f32[512,1]{0,1:T(1,128)S(1)} %bitcast.30), channel_id=1, replica_groups=mesh['dp'=8,'mp'=4] {'mp'}, use_global_device_ids=true, to_apply=%region_6.7 | all-reduce | flops 512 | bytes 4096 | tf_op jit(solution)/shard_map/psum | solution.py:379
  419.3 12.1 %reduce-scatter.3.cloned.1.call-done = bf16[512,1024]{1,0:T(8,128)(2,1)} async-done(((bf16[512,4096]{1,0:T(8,128)(2,1)}), bf16[512,1024]{1,0:T(8,128)(2,1)}) %reduce-scatter.3.cloned.1.call-update) | async-done | bytes 1048592 | tf_op jit(solution)/shard_map/reduce_scatter | solution.py:349
  431.4 4.4 fusion.7
  435.8 1.3 copy.39
  437.1 0.0 copy-done.11
  437.1 0.8 copy.40
  437.9 0.8 copy.41
  438.7 1.3 copy.42
  (35 shorter events, 0.1 us)
Async XLA Ops:
  9.8 9.8 %all-to-all-start = ((s32[8,1,3]{2,1,0:T(1,128)}), s32[8,1,3]{2,1,0:T(1,128)S(1)}, u32[]{:S(2)}, u32[]{:S(2)}) async-start(s32[8,1,3]{2,1,0:T(1,128)} %bitcast), calls=%async_computation | async-start | bytes 8192 | tf_op jit(solution)/shard_map/all_to_all | solution.py:326
  64.0 53.3 %copy-start.14 = (s32[8,2]{0,1:T(2,128)S(1)}, s32[8,2]{0,1:T(2,128)}, u32[]{:S(2)}) copy-start(s32[8,2]{0,1:T(2,128)} %param.14) | copy-start | bytes 196
  64.0 22.4 %all-to-all-start.1 = ((bf16[8,3,32,896]{3,2,1,0:T(8,128)(2,1)}), bf16[8,3,32,896]{3,2,1,0:T(8,128)(2,1)S(1)}, u32[]{:S(2)}, u32[]{:S(2)}) async-start(bf16[8,3,32,896]{3,2,1,0:T(8,128)(2,1)} %bitcast.28), calls=%async_computation.1 | async-start | bytes 2752512 | tf_op jit(solution)/shard_map/all_to_all | solution.py:331
  67.6 152.9 %all-gather.2.cloned.1.call-start = ((), (), s32[]{:S(2)}) async-start(), calls=%async_computation.4 | async-start | bytes 4587520 | tf_op jit(solution)/shard_map/all_gather | solution.py:334
  86.4 1.1 copy-start.7
  117.2 287.3 %reduce-scatter.5.cloned.1.call-start = ((), (), s32[]{:S(2)}) async-start(), calls=%async_computation.6 | async-start | bytes 5242880 | tf_op jit(solution)/shard_map/reduce_scatter | solution.py:375
  205.0 3.5 copy-start.12
  205.0 10.9 %slice-start = ((s8[8388608]{0:T(1024)(128)(4,1)}), s8[4194304]{0:T(1024)(128)(4,1)S(1)}, s32[]{:S(2)}) async-start(s8[8388608]{0:T(1024)(128)(4,1)} %bitcast.31), calls=%async_computation.7 | async-start | bytes 8388608
  208.4 7.4 %copy-start.5 = (bf16[512,4096]{1,0:T(8,128)(2,1)S(1)}, bf16[512,4096]{1,0:T(8,128)(2,1)}, u32[]{:S(2)}) copy-start(bf16[512,4096]{1,0:T(8,128)(2,1)} %param.10) | copy-start | bytes 12582916
  208.4 7.4 %slice-start.1 = ((s8[8388608]{0:T(1024)(128)(4,1)}), s8[4194304]{0:T(1024)(128)(4,1)S(1)}, s32[]{:S(2)}) async-start(s8[8388608]{0:T(1024)(128)(4,1)} %bitcast.31), calls=%async_computation.8 | async-start | bytes 8388608
  220.5 7.3 %copy-start.15 = (bf16[16,128,896]{2,1,0:T(8,128)(2,1)S(1)}, bf16[16,128,896]{2,1,0:T(8,128)(2,1)}, u32[]{:S(2)}) copy-start(bf16[16,128,896]{2,1,0:T(8,128)(2,1)} %all-gather.2.cloned.1.call-done) | copy-start | bytes 11010052
  220.5 7.3 %copy-start.17 = (bf16[896,1024]{1,0:T(8,128)(2,1)S(1)}, bf16[896,1024]{1,0:T(8,128)(2,1)}, u32[]{:S(2)}) copy-start(bf16[896,1024]{1,0:T(8,128)(2,1)} %get-tuple-element.20) | copy-start | bytes 5505028
  220.5 47.4 %slice-start.2 = ((s8[8388608]{0:T(1024)(128)(4,1)}), s8[4194304]{0:T(1024)(128)(4,1)S(1)}, s32[]{:S(2)}) async-start(s8[8388608]{0:T(1024)(128)(4,1)} %bitcast.33), calls=%async_computation.9 | async-start | bytes 8388608
  227.8 40.1 %slice-start.3 = ((s8[8388608]{0:T(1024)(128)(4,1)}), s8[4194304]{0:T(1024)(128)(4,1)S(1)}, s32[]{:S(2)}) async-start(s8[8388608]{0:T(1024)(128)(4,1)} %bitcast.33), calls=%async_computation.10 | async-start | bytes 8388608
  262.9 2.0 copy-start
  264.9 2.1 copy-start.2
  267.0 1.0 copy-start.3
  274.1 1.2 copy-start.4
  274.1 157.3 %reduce-scatter.3.cloned.1.call-start = ((), (), s32[]{:S(2)}) async-start(), calls=%async_computation.5 | async-start | bytes 5242880 | tf_op jit(solution)/shard_map/reduce_scatter | solution.py:349
  284.8 8.7 %copy-start.1 = (bf16[2048,1024]{1,0:T(8,128)(2,1)S(1)}, bf16[2048,1024]{1,0:T(8,128)(2,1)}, u32[]{:S(2)}) copy-start(bf16[2048,1024]{1,0:T(8,128)(2,1)} %copy-done) | copy-start | bytes 12582916
  284.8 8.7 %copy-start.16 = (bf16[16,128,896]{2,1,0:T(8,128)(2,1)S(1)}, bf16[16,128,896]{2,1,0:T(8,128)(2,1)}, u32[]{:S(2)}) copy-start(bf16[16,128,896]{2,1,0:T(8,128)(2,1)} %all-gather.2.cloned.1.call-done) | copy-start | bytes 11010052
  293.5 5.1 %copy-start.13 = (bf16[512,4096]{1,0:T(8,128)(2,1)S(1)}, bf16[512,4096]{1,0:T(8,128)(2,1)}, u32[]{:S(2)}) copy-start(bf16[512,4096]{1,0:T(8,128)(2,1)} %param.19) | copy-start | bytes 12582916
  298.6 6.7 %copy-start.6 = (bf16[512,4096]{1,0:T(8,128)(2,1)S(1)}, bf16[512,4096]{1,0:T(8,128)(2,1)}, u32[]{:S(2)}) copy-start(bf16[512,4096]{1,0:T(8,128)(2,1)} %param.10) | copy-start | bytes 12582916
  404.5 31.3 %copy-start.9 = (f32[512,1024]{1,0:T(8,128)S(1)}, f32[512,1024]{1,0:T(8,128)}, u32[]{:S(2)}) copy-start(f32[512,1024]{1,0:T(8,128)} %get-tuple-element.40) | copy-start | bytes 6291460
  431.4 5.7 %copy-start.11 = (f32[112,1024]{1,0:T(8,128)S(1)}, f32[112,1024]{1,0:T(8,128)}, u32[]{:S(2)}) copy-start(f32[112,1024]{1,0:T(8,128)} %get-tuple-element.41) | copy-start | bytes 1376260
  431.4 6.5 %copy-start.10 = (f32[112,1024]{1,0:T(8,128)S(1)}, f32[112,1024]{1,0:T(8,128)}, u32[]{:S(2)}) copy-start(f32[112,1024]{1,0:T(8,128)} %get-tuple-element.42) | copy-start | bytes 1376260
  435.8 2.9 copy-start.8
Sparse Core Ops, SparseCore 0:
  117.4 71.4 all-gather.1
  274.2 77.1 reduce-scatter.4
  353.8 77.5 reduce-scatter.2

commit v2 on v1

--- a/solution.py
+++ b/solution.py
@@ -109,7 +109,7 @@
         copy.wait_send()
 
 
-def gather_all(shards, axes):
+def gather_all(shards, axes, number):
     dp_count = lax.axis_size("dp")
     if dp_count != 8:
         return [lax.all_gather(s, "dp", axis=a, tiled=True) for s, a in zip(shards, axes)]
@@ -124,7 +124,10 @@
         out_specs=[ANY] * count,
         scratch_shapes=[pltpu.SemaphoreType.DMA((count, 14)), pltpu.SemaphoreType.DMA((count, 14)),
                         pltpu.SemaphoreType.DMA((count, 2))],
-        compiler_params=pltpu.CompilerParams(collective_id=0, has_side_effects=True),
+        compiler_params=pltpu.CompilerParams(collective_id=number, has_side_effects=True),
+        cost_estimate=pl.CostEstimate(
+            flops=0, transcendentals=0,
+            bytes_accessed=sum(40 * dp_count * s.size for s in shards)),
         name="gather_weights",
     )(*shards)
 
@@ -225,7 +228,7 @@
         + [pltpu.SemaphoreType.DMA((count, 10)), pltpu.SemaphoreType.DMA((count, 10)),
            pltpu.SemaphoreType.DMA((count, 4))],
         compiler_params=pltpu.CompilerParams(
-            collective_id=1, has_side_effects=True, vmem_limit_bytes=56 * 2**20),
+            collective_id=2, has_side_effects=True, vmem_limit_bytes=56 * 2**20),
         name="scatter_gradients",
     )(*parts)
 
@@ -248,7 +251,7 @@
         functools.partial(pick_kernel, count, span),
         out_shape=jax.ShapeDtypeStruct((count, span, source.shape[2]), source.dtype),
         in_specs=[pl.BlockSpec(memory_space=pltpu.SMEM), ANY],
-        out_specs=ANY,
+        out_specs=pl.BlockSpec(memory_space=pltpu.VMEM),
         scratch_shapes=[pltpu.SemaphoreType.DMA((count,))],
         name="pick_blocks",
     )(table, source)
@@ -328,14 +331,16 @@
     span = block_len // mp_count
     picked = pick(cache, picked_rows.reshape(-1), mp_place, span)
     picked = picked.reshape(dp_count, CAP, span, enc_width)
+    picked, w_out = lax.optimization_barrier((picked, w_out))
+    (output_full,) = gather_all((w_out,), (1,), 0)
     arrived = lax.all_to_all(picked, "dp", split_axis=0, concat_axis=0, tiled=True)
+    arrived, output_full = lax.optimization_barrier((arrived, output_full))
     arrived = arrived.reshape(dp_count * CAP, span, enc_width)
     chosen = pick(arrived, slot_of, jnp.int32(0), span)
+    chosen, w_query = lax.optimization_barrier((chosen, w_query))
     blocks = lax.all_gather(chosen, "mp", axis=1, tiled=True)
     flat_blocks = blocks.reshape(request_count * block_len, enc_width)
-    query_full, output_full, key_full, value_full = gather_all(
-        (w_query, w_out, w_key, w_value), (0, 1, 0, 0)
-    )
+    query_full, key_full, value_full = gather_all((w_query, w_key, w_value), (0, 0, 0), 1)
     queries = jnp.dot(normed, query_full, preferred_element_type=jnp.float32).astype(jnp.bfloat16)
     grad_attn = jnp.einsum(
         "td,sd->ts", grad_out, output_full, preferred_element_type=jnp.float32

time: 447 us -> 385 us (0.86)
  Pallas kernels: 284 us -> 238 us
  waiting for transfers between devices: 35 us -> 17.3 us
    pallas_call x2, Pallas kernels: 73.4 us -> 6.43 us  [pick(): pl.pallas_call(functools.partial(pick_kernel, count, span), out_shape=jax...]
    pallas_call x1 -> x2, Pallas kernels: 87.6 us -> 109 us  [gather_all(): pl.pallas_call(functools.partial(gather_kernel, axes, shapes), out_shape=...]
    all_to_all x1, waiting for transfers between devices: 18.2 us -> 0.01 us  [on_device(): lax.all_to_all(picked, 'dp', split_axis=0, concat_axis=0, tiled=True)]
    unnamed x50 -> x46, local copies, waits for them, and re-layouts: 12.5 us -> 12.3 us
  transfers between devices with their start and end apart: 5 -> 5, of which waited for: 3 -> 3; matrix products, arithmetic and copies ran while one was open for 12% -> 15% of each run, Pallas kernels for 40% -> 52%
where the time goes in v2:
time: 385 us; the launch traced here: 384 us
  Pallas kernels  238 us (62%)
  matrix products  69 us (18%)
  waiting for transfers between devices  17.3 us (4%)
  between operations  14 us (4%)
  local copies, waits for them, and re-layouts  13.3 us (3%)
  other arithmetic  11.9 us (3%)
  blocking collectives  11.5 us (3%)
  starting transfers between devices  8.88 us (2%)
    pallas_call x2, Pallas kernels, gather_all(): pl.pallas_call(functools.partial(gather_kernel, axes, shapes), out_shape=...  109 us
    pallas_call x1, Pallas kernels, scatter_all(): pl.pallas_call(functools.partial(scatter_kernel, axes, shapes), out_shape...  92.8 us
    pallas_call x1, Pallas kernels, attend(): pl.pallas_call(functools.partial(attend_kernel, width // HD, block_len),...  30.1 us
    unnamed x46, local copies, waits for them, and re-layouts  12.3 us
    reduce_scatter x1, waiting for transfers between devices, on_device(): lax.psum_scatter(partial_out.astype(jnp.bfloat16), 'mp', scatter_dimensio...  11.9 us
    psum x1, blocking collectives, on_device(): stat_rows = lax.psum(stat_part, 'mp') / width  11.5 us
    dot_general x1, matrix products, on_device(): jnp.dot(attended, output_full, preferred_element_type=jnp.float32)  9.47 us
    dot_general x1, matrix products, on_device(): jnp.einsum('td,sd->ts', grad_out, output_full, preferred_element_type=jnp...  9.24 us
  transfers between devices with their start and end apart: 5, of which 3 were waited for; matrix products, arithmetic and copies ran while one was open for 15% of the time, Pallas kernels for 52%

profile of v2, /device:TPU:0, one launch (start us, length us, event | category | flops | bytes accessed | tf_op | source)
XLA Modules:
  0.0 383.9 jit_solution(8188710791117788803)
XLA Ops:
  7.2 0.7 broadcast_add_fusion
  7.8 0.1 copy.30
  7.9 0.1 add.60
  8.0 0.8 copy.29
  8.8 0.1 reshape.75
  8.9 0.2 convert_reduce_fusion
  9.0 0.1 select_reduce_fusion
  9.1 0.7 sub.9
  9.8 5.2 %all-to-all-start = ((s32[8,1,3]{2,1,0:T(1,128)}), s32[8,1,3]{2,1,0:T(1,128)S(1)}, u32[]{:S(2)}, u32[]{:S(2)}) async-start(s32[8,1,3]{2,1,0:T(1,128)} %bitcast), calls=%async_computation | async-start | bytes 8192 | tf_op jit(solution)/shard_map/all_to_all | solution.py:329
  15.0 4.6 %all-to-all-done = s32[8,1,3]{2,1,0:T(1,128)S(1)} async-done(((s32[8,1,3]{2,1,0:T(1,128)}), s32[8,1,3]{2,1,0:T(1,128)S(1)}, u32[]{:S(2)}, u32[]{:S(2)}) %all-to-all-start) | async-done | bytes 128 | tf_op jit(solution)/shard_map/all_to_all | solution.py:329
  19.6 0.1 min.12
  19.7 0.6 pad_add_fusion.1.ids
  20.3 3.5 pick_blocks.2
  23.8 3.6 all-to-all-start.1
  27.4 0.0 all-gather.2.cloned.1.call-start
  27.4 0.6 pad_add_fusion.ids
  28.0 54.0 %gather_weights.2 = bf16[1024,4096]{1,0:T(8,128)(2,1)} custom-call(bf16[1024,512]{1,0:T(8,128)(2,1)} %refs_0_), custom_call_target="tpu_custom_call" | custom-call | bytes 167772160 | tf_op jit(solution)/shard_map/gather_weights/pallas_call | solution.py:120
  82.0 0.0 all-to-all-done.1
  82.0 0.0 copy-start.7
  82.0 1.1 copy-done.7
  83.1 2.9 pick_blocks.3
  86.0 0.0 all-gather.2.cloned.1.call-update
  86.0 0.0 reduce-scatter.5.cloned.1.call-start
  86.1 0.0 copy-done.13
  86.1 0.1 copy.33.lens
  86.2 3.1 fusion
  89.3 54.8 %gather_weights.3 = (bf16[4096,1024]{1,0:T(8,128)(2,1)}, bf16[896,1024]{1,0:T(8,128)(2,1)}, bf16[896,1024]{1,0:T(8,128)(2,1)}) custom-call(bf16[512,1024]{1,0:T(8,128)(2,1)} %refs_0_.1, bf16[112,1024]{1,0:T(8,128)(2,1)} %refs_1_.1, bf16[112,1024]{1,0:T(8,128)(2,1)} %refs_2_.1), custom_call_target="tpu_custom_call" | custom-call | bytes 241172480 | tf_op jit(solution)/shard_map/gather_weights/pallas_call | solution.py:120
  144.1 0.0 copy-start.5
  144.1 9.2 %fusion.14.g_ref = bf16[512,1024]{1,0:T(8,128)(2,1)S(1)} fusion(bf16[1024,4096]{1,0:T(8,128)(2,1)} %gather_weights.2, bf16[512,4096]{1,0:T(8,128)(2,1)} %param.19), kind=kOutput, calls=%fused_computation.25 | convolution fusion | flops 4295491584 | bytes 13631488 | tf_op jit(solution)/shard_map/td,sd->ts/dot_general | solution.py:345
  153.4 0.0 copy-done.5
  153.4 0.0 copy-done.14
  153.4 4.6 %fusion.11.q_ref = bf16[512,1024]{1,0:T(8,128)(2,1)S(1)} fusion(bf16[4096,1024]{1,0:T(8,128)(2,1)S(1)} %copy-done.14, bf16[512,4096]{1,0:T(8,128)(2,1)S(1)} %copy-done.5, f32[512]{0:T(512)S(1)} %add_rsqrt_fusion), kind=kOutput, calls=%fused_computation.23 | convolution fusion | flops 4301783040 | bytes 13633536 | tf_op jit(solution)/shard_map/dot_general | solution.py:344
  158.0 0.7 all-gather.2.cloned.1.call-done
  158.7 7.5 %convolution_convert_fusion.5.k_ref = bf16[2048,1024]{1,0:T(8,128)(2,1)S(1)} fusion(bf16[2048,896]{1,0:T(8,128)(2,1)} %bitcast.33, bf16[896,1024]{1,0:T(8,128)(2,1)} %get-tuple-element.29), kind=kOutput, calls=%fused_computation.9 | convolution fusion | flops 3760193536 | bytes 9699328 | tf_op jit(solution)/shard_map/dot_general | solution.py:348
  166.2 0.0 slice-start.1
  166.2 4.7 %convolution_convert_fusion.4.v_ref = bf16[2048,1024]{1,0:T(8,128)(2,1)S(1)} fusion(bf16[2048,896]{1,0:T(8,128)(2,1)S(1)} %bitcast.35, bf16[896,1024]{1,0:T(8,128)(2,1)S(1)} %copy-done.17), kind=kOutput, calls=%fused_computation.8 | convolution fusion | flops 3760193536 | bytes 9699328 | tf_op jit(solution)/shard_map/dot_general | solution.py:349
  170.9 30.1 %attend.1 = (bf16[512,1024]{1,0:T(8,128)(2,1)S(1)}, bf16[512,1024]{1,0:T(8,128)(2,1)S(1)}, bf16[2048,1024]{1,0:T(8,128)(2,1)S(1)}, bf16[2048,1024]{1,0:T(8,128)(2,1)S(1)}) custom-call(s32[8,2]{1,0:T(8,128)S(1)} %copy.33.lens, bf16[512,1024]{1,0:T(8,128)(2,1)S(1)} %fusion.11.q_ref, bf16[2048,1024]{1,0:T(8,128)(2,1)S(1)} %convolution_convert_fusion.5.k_ref, ...), custom_call_target="tpu_custom_call" | custom-call | tf_op jit(solution)/shard_map/attend/pallas_call | solution.py:293
  201.0 0.0 copy-start
  201.0 2.0 copy-done
  203.1 2.0 copy-done.2
  205.1 1.0 copy-done.3
  206.1 6.1 %convolution_convert_fusion.2 = bf16[512,4096]{1,0:T(8,128)(2,1)} fusion(bf16[512,1024]{1,0:T(8,128)(2,1)S(1)} %get-tuple-element.33, bf16[4096,1024]{1,0:T(8,128)(2,1)S(1)} %bitcast.32), kind=kOutput, calls=%fused_computation.6 | convolution fusion | flops 4297064448 | bytes 13631488 | tf_op jit(solution)/shard_map/ts,ds->td/dot_general | solution.py:373
  212.2 0.0 reduce-scatter.5.cloned.1.call-update
  212.2 0.0 reduce-scatter.3.cloned.1.call-start
  212.2 1.1 copy-done.4
  213.4 9.5 %convolution_convert_fusion.3 = bf16[512,4096]{1,0:T(8,128)(2,1)} fusion(bf16[512,1024]{1,0:T(8,128)(2,1)S(1)} %copy-done.4, bf16[1024,4096]{1,0:T(8,128)(2,1)} %gather_weights.2), kind=kOutput, calls=%fused_computation.7 | convolution fusion | flops 4297064448 | bytes 13631488 | tf_op jit(solution)/shard_map/dot_general | solution.py:353
  222.8 0.0 reduce-scatter.3.cloned.1.call-update
  222.9 8.7 %convolution_convert_fusion.7.refs_2_ = bf16[896,1024]{1,0:T(8,128)(2,1)} fusion(bf16[2048,896]{1,0:T(8,128)(2,1)} %bitcast.34, bf16[2048,1024]{1,0:T(8,128)(2,1)} %copy-done.2), kind=kOutput, calls=%fused_computation.21 | convolution fusion | flops 3759013888 | bytes 9699328 | tf_op jit(solution)/shard_map/re,rs->es/dot_general | solution.py:363
  231.6 0.0 copy-done.16
  231.6 5.1 %convolution_convert_fusion.6.refs_3_ = bf16[896,1024]{1,0:T(8,128)(2,1)} fusion(bf16[2048,896]{1,0:T(8,128)(2,1)S(1)} %bitcast.36, bf16[2048,1024]{1,0:T(8,128)(2,1)S(1)} %copy-done.1), kind=kOutput, calls=%fused_computation.20 | convolution fusion | flops 3759013888 | bytes 9699328 | tf_op jit(solution)/shard_map/re,rs->es/dot_general | solution.py:366
  236.7 6.7 %convolution_convert_fusion.refs_1_ = bf16[1024,4096]{1,0:T(8,128)(2,1)} fusion(bf16[512,1024]{1,0:T(8,128)(2,1)S(1)} %copy-done.4, bf16[512,4096]{1,0:T(8,128)(2,1)S(1)} %copy-done.12), kind=kOutput, calls=%fused_computation.4 | convolution fusion | flops 4299161600 | bytes 13631488 | tf_op jit(solution)/shard_map/ts,td->sd/dot_general | solution.py:361
  243.4 6.9 %convolution_convert_fusion.1.refs_0_ = bf16[4096,1024]{1,0:T(8,128)(2,1)} fusion(bf16[512,1024]{1,0:T(8,128)(2,1)S(1)} %get-tuple-element.33, bf16[512,4096]{1,0:T(8,128)(2,1)S(1)} %copy-done.6, f32[512]{0:T(512)S(1)} %add_rsqrt_fusion), kind=kOutput, calls=%fused_computation.5 | convolution fusion | flops 4305453056 | bytes 13633536 | tf_op jit(solution)/shard_map/td,ts->ds/dot_general | solution.py:362
  250.3 92.8 %scatter_gradients.1 = (f32[512,1024]{1,0:T(8,128)}, f32[1024,512]{1,0:T(8,128)}, f32[112,1024]{1,0:T(8,128)}, f32[112,1024]{1,0:T(8,128)}) custom-call(bf16[4096,1024]{1,0:T(8,128)(2,1)} %convolution_convert_fusion.1.refs_0_, bf16[1024,4096]{1,0:T(8,128)(2,1)} %convolution_convert_fusion.refs_1_, bf16[896,1024]{1,0:T(8,128)(2,1)} %convolution_convert_fusion.7.refs_2_, ...), custom_call_target="tpu_custom_call" | custom-call | tf_op jit(solution)/shard_map/scatter_gradients/pallas_call | solution.py:222
  343.1 0.0 copy-start.9
  343.1 0.0 reduce-scatter.5.cloned.1.call-done
  343.1 2.2 fusion.4
  345.4 11.5 %psum.7 = f32[512,1]{0,1:T(1,128)S(1)} all-reduce(f32[512,1]{0,1:T(1,128)S(1)} %bitcast.30), channel_id=1, replica_groups=mesh['dp'=8,'mp'=4] {'mp'}, use_global_device_ids=true, to_apply=%region_6.7 | all-reduce | flops 512 | bytes 4096 | tf_op jit(solution)/shard_map/psum | solution.py:384
  356.9 11.9 %reduce-scatter.3.cloned.1.call-done = bf16[512,1024]{1,0:T(8,128)(2,1)} async-done(((bf16[512,4096]{1,0:T(8,128)(2,1)}), bf16[512,1024]{1,0:T(8,128)(2,1)}) %reduce-scatter.3.cloned.1.call-update) | async-done | bytes 1048592 | tf_op jit(solution)/shard_map/reduce_scatter | solution.py:354
  368.8 4.4 %fusion.7 = (bf16[512,1024]{1,0:T(8,128)(2,1)}, bf16[512,1024]{1,0:T(8,128)(2,1)}) fusion(bf16[512,1024]{1,0:T(8,128)(2,1)} %reduce-scatter.5.cloned.1.call-done, f32[512]{0:T(512)S(1)} %bitcast.29, f32[512]{0:T(512)S(1)} %add_rsqrt_fusion, bf16[512,4096]{1,0:T(8,128)(2,1)} %param.19, s32[]{:T(128)S(6)} %select_n.4, bf16[512,4096]{1,0:T(8,128)(2,1)} %param.10, ...), kind=kLoop, calls=%fused_computation.19 | loop fusion | flops 6291456 | bytes 6295556 | tf_op jit(solution)/shard_map/convert_element_type | solution.py:386
  373.2 1.3 copy.39
  374.5 0.0 copy-done.11
  374.5 0.8 copy.40
  375.3 0.8 copy.41
  376.1 1.3 copy.42
  (31 shorter events, 0.1 us)
Async XLA Ops:
  9.8 9.8 %all-to-all-start = ((s32[8,1,3]{2,1,0:T(1,128)}), s32[8,1,3]{2,1,0:T(1,128)S(1)}, u32[]{:S(2)}, u32[]{:S(2)}) async-start(s32[8,1,3]{2,1,0:T(1,128)} %bitcast), calls=%async_computation | async-start | bytes 8192 | tf_op jit(solution)/shard_map/all_to_all | solution.py:329
  23.8 58.2 %all-to-all-start.1 = ((bf16[8,3,32,896]{3,2,1,0:T(8,128)(2,1)}), bf16[8,3,32,896]{3,2,1,0:T(8,128)(2,1)S(1)}, u32[]{:S(2)}, u32[]{:S(2)}) async-start(bf16[8,3,32,896]{3,2,1,0:T(8,128)(2,1)} %bitcast.28), calls=%async_computation.1 | async-start | bytes 2752512 | tf_op jit(solution)/shard_map/all_to_all | solution.py:336
  27.4 131.3 %all-gather.2.cloned.1.call-start = ((), (), s32[]{:S(2)}) async-start(), calls=%async_computation.4 | async-start | bytes 4587520 | tf_op jit(solution)/shard_map/all_gather | solution.py:341
  28.0 58.1 %copy-start.13 = (s32[8,2]{0,1:T(2,128)S(1)}, s32[8,2]{0,1:T(2,128)}, u32[]{:S(2)}) copy-start(s32[8,2]{0,1:T(2,128)} %param.14) | copy-start | bytes 196
  82.0 1.1 copy-start.7
  86.0 257.1 %reduce-scatter.5.cloned.1.call-start = ((), (), s32[]{:S(2)}) async-start(), calls=%async_computation.6 | async-start | bytes 5242880 | tf_op jit(solution)/shard_map/reduce_scatter | solution.py:380
  144.1 9.3 %copy-start.5 = (bf16[512,4096]{1,0:T(8,128)(2,1)S(1)}, bf16[512,4096]{1,0:T(8,128)(2,1)}, u32[]{:S(2)}) copy-start(bf16[512,4096]{1,0:T(8,128)(2,1)} %param.10) | copy-start | bytes 12582916
  144.1 9.3 %copy-start.14 = (bf16[4096,1024]{1,0:T(8,128)(2,1)S(1)}, bf16[4096,1024]{1,0:T(8,128)(2,1)}, u32[]{:S(2)}) copy-start(bf16[4096,1024]{1,0:T(8,128)(2,1)} %get-tuple-element.27) | copy-start | bytes 25165828
  158.7 7.5 %copy-start.15 = (bf16[16,128,896]{2,1,0:T(8,128)(2,1)S(1)}, bf16[16,128,896]{2,1,0:T(8,128)(2,1)}, u32[]{:S(2)}) copy-start(bf16[16,128,896]{2,1,0:T(8,128)(2,1)} %all-gather.2.cloned.1.call-done) | copy-start | bytes 11010052
  158.7 7.5 %copy-start.17 = (bf16[896,1024]{1,0:T(8,128)(2,1)S(1)}, bf16[896,1024]{1,0:T(8,128)(2,1)}, u32[]{:S(2)}) copy-start(bf16[896,1024]{1,0:T(8,128)(2,1)} %get-tuple-element.30) | copy-start | bytes 5505028
  158.7 47.4 %slice-start = ((s8[8388608]{0:T(1024)(128)(4,1)}), s8[4194304]{0:T(1024)(128)(4,1)S(1)}, s32[]{:S(2)}) async-start(s8[8388608]{0:T(1024)(128)(4,1)} %bitcast.31), calls=%async_computation.7 | async-start | bytes 8388608
  166.2 39.9 %slice-start.1 = ((s8[8388608]{0:T(1024)(128)(4,1)}), s8[4194304]{0:T(1024)(128)(4,1)S(1)}, s32[]{:S(2)}) async-start(s8[8388608]{0:T(1024)(128)(4,1)} %bitcast.31), calls=%async_computation.8 | async-start | bytes 8388608
  201.0 2.0 copy-start
  203.1 2.0 copy-start.2
  205.1 1.0 copy-start.3
  212.2 1.2 copy-start.4
  212.2 156.6 %reduce-scatter.3.cloned.1.call-start = ((), (), s32[]{:S(2)}) async-start(), calls=%async_computation.5 | async-start | bytes 5242880 | tf_op jit(solution)/shard_map/reduce_scatter | solution.py:354
  222.9 8.7 %copy-start.1 = (bf16[2048,1024]{1,0:T(8,128)(2,1)S(1)}, bf16[2048,1024]{1,0:T(8,128)(2,1)}, u32[]{:S(2)}) copy-start(bf16[2048,1024]{1,0:T(8,128)(2,1)} %copy-done) | copy-start | bytes 12582916
  222.9 8.7 %copy-start.16 = (bf16[16,128,896]{2,1,0:T(8,128)(2,1)S(1)}, bf16[16,128,896]{2,1,0:T(8,128)(2,1)}, u32[]{:S(2)}) copy-start(bf16[16,128,896]{2,1,0:T(8,128)(2,1)} %all-gather.2.cloned.1.call-done) | copy-start | bytes 11010052
  231.6 5.1 %copy-start.12 = (bf16[512,4096]{1,0:T(8,128)(2,1)S(1)}, bf16[512,4096]{1,0:T(8,128)(2,1)}, u32[]{:S(2)}) copy-start(bf16[512,4096]{1,0:T(8,128)(2,1)} %param.19) | copy-start | bytes 12582916
  236.7 6.7 %copy-start.6 = (bf16[512,4096]{1,0:T(8,128)(2,1)S(1)}, bf16[512,4096]{1,0:T(8,128)(2,1)}, u32[]{:S(2)}) copy-start(bf16[512,4096]{1,0:T(8,128)(2,1)} %param.10) | copy-start | bytes 12582916
  343.1 30.1 %copy-start.9 = (f32[512,1024]{1,0:T(8,128)S(1)}, f32[512,1024]{1,0:T(8,128)}, u32[]{:S(2)}) copy-start(f32[512,1024]{1,0:T(8,128)} %get-tuple-element.50) | copy-start | bytes 6291460
  368.8 5.7 %copy-start.11 = (f32[112,1024]{1,0:T(8,128)S(1)}, f32[112,1024]{1,0:T(8,128)}, u32[]{:S(2)}) copy-start(f32[112,1024]{1,0:T(8,128)} %get-tuple-element.51) | copy-start | bytes 1376260
  368.8 6.5 %copy-start.10 = (f32[112,1024]{1,0:T(8,128)S(1)}, f32[112,1024]{1,0:T(8,128)}, u32[]{:S(2)}) copy-start(f32[112,1024]{1,0:T(8,128)} %get-tuple-element.52) | copy-start | bytes 1376260
  373.2 2.9 copy-start.8
Sparse Core Ops, SparseCore 0:
  86.2 72.4 all-gather.1
  212.3 76.5 reduce-scatter.4
  291.3 77.5 reduce-scatter.2
